TPU v7x, 32 devices: a whole 2x2x4 slice. The times are simulated.
32 devices in a mesh: rows: 4 (over y, x), feat: 8 (over z, core).
Axes of the slice: x: 2, y: 2, z: 4, core: 2. Of those that a mesh axis runs over, the one named last changes fastest.
Arguments:
- scores: float32 [32768], P('rows'), may hold values from -6 to 6
- query_ids: int32 [32768], P('rows'), may hold values from 0 to 203, never falling along the last dimension, each value on 1 to 512 neighbouring positions
- positions: int32 [32768], P('rows'), may hold values from 0 to 31
- clicks: int32 [32768], P('rows'), may hold values from 0 to 1
- nodes: int32 [32768], P('rows'), may hold values from 0 to 3
- bins: int32 [1024, 32768], P('feat', 'rows'), may hold values from 0 to 255
Outputs:
- bias_ratios: float32 [2, 32], replicated
- grad_hess: bfloat16 [2, 32768], P(None, 'rows')
- node_hist: float32 [256, 3, 4, 1024], P('rows', None, None, 'feat')
- parent_hist: float32 [256, 3, 2, 1024], P('rows', None, None, 'feat')
Inputs may be any that keep to these rules, and one draw needn't show every extreme that they name: `query_ids`: each query's documents are consecutive rows, in increasing query order; a query holds 1 to 512 documents, and some query holds exactly 512.
All inputs are finite; a program needn't handle non-finite values.
Results may differ from a plain program's by a relative error of at most 0.0015.
Values may be sent and summed in bfloat16 or wider, within the bound.
A program may use at most 64 MiB of HBM per device.

v0:
```python
import math

import jax
import jax.numpy as jnp
from jax import lax
from jax.sharding import PartitionSpec as P

BINS = 256
P_SIZE = 32
NODES = 4
MAXQ = 512


eps = 1e-06


def extended_2(cells, sides, width):
    for axis, dim in sides:
        count = lax.axis_size(axis)
        ends = count - 1
        head = lax.slice_in_dim(cells, 0, width, axis=dim)
        tail = lax.slice_in_dim(cells, cells.shape[dim] - width, cells.shape[dim], axis=dim)
        cells = jnp.concatenate(
            [
                lax.ppermute(tail, axis, [(i, (i + 1) % count) for i in range(ends)]),
                cells,
                lax.ppermute(head, axis, [((i + 1) % count, i) for i in range(ends)]),
            ],
            axis=dim,
        )
    return cells


def discount(place):
    return jnp.log(2.0) / jnp.log(2.0 + place)


def precise_dot(left, right):
    return jnp.dot(left, right, precision=lax.Precision.HIGHEST)


def place_table(place):
    return (place[:, None] == jnp.arange(P_SIZE, dtype=jnp.float32)[None, :]).astype(jnp.float32)


def pair_terms(own_rows, window):
    same_query = jnp.logical_and(
        own_rows[1][:, None] == window[1][None, :], window[1][None, :] > 0.5
    ).astype(jnp.float32)
    clicked = jnp.sum(same_query * window[2][None, :], axis=1)
    rank_values = jnp.arange(MAXQ, dtype=jnp.float32)
    ideal_gain = jnp.sum(
        jnp.where(rank_values[None, :] < clicked[:, None], discount(rank_values)[None, :], 0.0),
        axis=1,
    )
    ideal_gain = jnp.maximum(ideal_gain, 1.0)
    spread = own_rows[0][:, None] - window[0][None, :]
    change = (
        jnp.abs(discount(own_rows[3])[:, None] - discount(window[3])[None, :]) / ideal_gain[:, None]
    )
    forward = same_query * own_rows[2][:, None] * (1.0 - window[2])[None, :]
    backward = same_query * (1.0 - own_rows[2])[:, None] * window[2][None, :]
    return (spread, change, forward, backward)


def bias_ratio(sums):
    middle = jnp.mean(sums)
    return (sums + middle + eps) / (2.0 * middle + eps)


def lambdas(spread, change, forward, backward, own_table, far_table, plus_ratio, minus_ratio):
    plus_own = precise_dot(own_table, plus_ratio)
    minus_own = precise_dot(own_table, minus_ratio)
    plus_far = precise_dot(far_table, plus_ratio)
    minus_far = precise_dot(far_table, minus_ratio)
    weight_fwd = change * forward / (plus_own[:, None] * minus_far[None, :])
    weight_bwd = change * backward / (plus_far[None, :] * minus_own[:, None])
    ahead_prob = jax.nn.sigmoid(-spread)
    gradient = jnp.sum((1.0 - ahead_prob) * weight_bwd - ahead_prob * weight_fwd, axis=1)
    hessian = jnp.sum(ahead_prob * (1.0 - ahead_prob) * (weight_fwd + weight_bwd), axis=1)
    return jnp.stack([gradient, hessian]).astype(jnp.bfloat16)


def node_columns(channels, member_ids, node_count):
    member = (member_ids[None, :] == jnp.arange(node_count, dtype=jnp.int32)[:, None]).astype(
        jnp.bfloat16
    )
    return (channels[:, None, :] * member[None, :, :]).reshape(3 * node_count, -1)


def bin_term(bins, columns, amount):
    levels = jnp.arange(amount, dtype=jnp.int32)
    feature_count, row_count = bins.shape
    stride = math.gcd(1024, row_count)
    block_count = row_count // stride
    column_count = columns.shape[0]
    bin_blocks = bins.reshape(feature_count, block_count, stride).transpose(1, 0, 2)
    column_blocks = columns.reshape(column_count, block_count, stride).transpose(1, 0, 2)

    def add_block(running, pieces):
        bin_piece, column_piece = pieces
        onehot = (bin_piece[:, None, :] == levels[None, :, None]).astype(jnp.bfloat16)
        return (
            running
            + jnp.einsum("fkr,cr->kcf", onehot, column_piece, preferred_element_type=jnp.float32),
            None,
        )

    start_value = jnp.zeros((amount, column_count, feature_count), jnp.float32)
    running, _ = lax.scan(add_block, start_value, (bin_blocks, column_blocks))
    return running


def exact_planes(scores, query_ids, positions, clicks):
    query_plus = query_ids + 1
    score_high = scores.astype(jnp.bfloat16)
    remainder = scores - score_high.astype(jnp.float32)
    score_mid = remainder.astype(jnp.bfloat16)
    score_low = (remainder - score_mid.astype(jnp.float32)).astype(jnp.bfloat16)
    id_high = (query_plus // 256).astype(jnp.bfloat16)
    id_low = (query_plus % 256).astype(jnp.bfloat16)
    return jnp.stack(
        [
            score_high,
            score_mid,
            score_low,
            id_high,
            id_low,
            clicks.astype(jnp.bfloat16),
            positions.astype(jnp.bfloat16),
        ]
    )


def per_device(scores, query_ids, positions, clicks, nodes, bins):
    rows_dev = scores.shape[0]
    block_rows = rows_dev // lax.axis_size("feat")
    feature_count = bins.shape[0]
    bins_dev = BINS // lax.axis_size("rows")
    packed = jnp.stack(
        [
            scores,
            (query_ids + 1).astype(jnp.float32),
            clicks.astype(jnp.float32),
            positions.astype(jnp.float32),
        ]
    )
    outgoing = exact_planes(scores, query_ids, positions, clicks)
    arrived = extended_2(outgoing, (("rows", 1),), MAXQ).astype(jnp.float32)
    extended = jnp.stack(
        [
            arrived[0] + arrived[1] + arrived[2],
            arrived[3] * 256.0 + arrived[4],
            arrived[5],
            arrived[6],
        ]
    )
    first_row = lax.axis_index("feat") * block_rows
    own_rows = lax.dynamic_slice_in_dim(packed, first_row, block_rows, 1)
    window = lax.dynamic_slice_in_dim(extended, first_row, block_rows + 2 * MAXQ, 1)
    spread, change, forward, backward = pair_terms(own_rows, window)
    losses = jax.nn.softplus(-spread) * change * forward
    own_table = place_table(own_rows[3])
    far_table = place_table(window[3])
    totals = lax.psum(precise_dot(own_table.T, precise_dot(losses, far_table)), ("rows", "feat"))
    plus_ratio = bias_ratio(jnp.sum(totals, axis=1))
    minus_ratio = bias_ratio(precise_dot(1.0 / plus_ratio, totals))
    pieces = lambdas(
        spread, change, forward, backward, own_table, far_table, plus_ratio, minus_ratio
    )
    grad_hess = lax.all_gather(pieces, "feat", axis=1, tiled=True)
    channels = jnp.concatenate([grad_hess, jnp.ones((1, rows_dev), jnp.bfloat16)], axis=0)
    columns = jnp.concatenate(
        [node_columns(channels, nodes, NODES), node_columns(channels, nodes // 2, NODES // 2)],
        axis=0,
    )
    summed = lax.psum_scatter(
        bin_term(bins, columns, bins_dev * lax.axis_size("rows")).astype(jnp.bfloat16),
        "rows",
        scatter_dimension=0,
        tiled=True,
    ).astype(jnp.float32)
    node_hist = summed[:, : 3 * NODES].reshape(-1, 3, NODES, feature_count)
    parent_hist = summed[:, 3 * NODES :].reshape(-1, 3, NODES // 2, feature_count)
    bias_ratios = jnp.stack([plus_ratio, minus_ratio])
    return (bias_ratios, grad_hess, node_hist, parent_hist)


def solution(mesh):
    return jax.shard_map(
        per_device,
        mesh=mesh,
        in_specs=(P("rows"), P("rows"), P("rows"), P("rows"), P("rows"), P("feat", "rows")),
        out_specs=(
            P(),
            P(None, "rows"),
            P("rows", None, None, "feat"),
            P("rows", None, None, "feat"),
        ),
        check_vma=False,
    )
```

profile of v0, /device:TPU:0, one launch (start us, length us, event | category | flops | bytes accessed | tf_op | source)
XLA Modules:
  0.0 361.5 jit_solution(18394283134385340247)
XLA Ops:
  11.1 4.8 %collective-permute-start = (bf16[7,512]{1,0:T(8,128)(2,1)S(1)}, bf16[7,512]{1,0:T(8,128)(2,1)S(1)}, u32[]{:S(2)}, u32[]{:S(2)}) collective-permute-start(bf16[7,512]{1,0:T(8,128)(2,1)S(1)} %get-tuple-element.79), channel_id=1, source_target_pairs={{0,8},{8,16},{16,24},{1,9},{9,17},{17,25},{2,10},{10,18},{18,26},{... | collective-permute-start | bytes 21512 | tf_op jit(solution)/shard_map/ppermute | solution.py:25
  15.9 1.3 collective-permute-start.1
  19.7 5.6 %copy.18 = s32[128,8192]{0,1:T(8,128)} copy(s32[128,8192]{1,0:T(8,128)} %param.13) | data formatting | bytes 8388608 | tf_op args[5]
  25.7 1.8 select_reduce_fusion
  27.9 12.0 %fusion.21 = f32[1024,32]{0,1:T(8,128)S(1)} fusion(f32[2048]{0:T(1024)S(1)} %bitcast.80, f32[1024]{0:T(1024)S(1)} %bitcast.72, f32[1024]{0:T(1024)S(1)} %get-tuple-element.104, f32[2048]{0:T(1024)S(1)} %bitcast.83, f32[2048]{0:T(1024)S(1)} %bitcast.78, f32[1024]{0:T(1024)S(1)} %get-tuple-element.103, f32[2048]{0:T(1024)S(1)} %bitcast.85, ...), kind=kOutput, calls=%fused_computation.33 | convolution fusion | flops 841023488 | bytes 194560 | tf_op jit(solution)/shard_map/dot_general | solution.py:39
  40.5 41.8 %psum.7 = f32[32,32]{1,0:T(8,128)S(1)} all-reduce(f32[32,32]{1,0:T(8,128)S(1)} %fusion.42), channel_id=1, replica_groups=mesh['rows'=4,'feat'=8] {'rows','feat'}, use_global_device_ids=true, to_apply=%region_2.3 | all-reduce | flops 1024 | bytes 8192 | tf_op jit(solution)/shard_map/psum | solution.py:165
  88.6 12.1 %fusion.18 = (bf16[1024]{0:T(1024)(128)(2,1)S(1)}, bf16[1024]{0:T(1024)(128)(2,1)S(1)}) fusion(f32[2048]{0:T(1024)S(1)} %bitcast.86, f32[1024]{0:T(1024)S(1)} %bitcast.93, f32[1024]{0:T(1024)S(1)} %bitcast.99, f32[2048]{0:T(1024)S(1)} %bitcast.98, f32[2048]{0:T(1024)S(1)} %bitcast.88, f32[1024]{0:T(1024)S(1)} %broadcast_subtract_fusion.1, ...), kind=kLoop, calls=%fused_computation.25 | loop fusion | flops 56621056 | bytes 96256 | tf_op jit(solution)/shard_map/reduce_sum | solution.py:79
  100.7 14.0 %all_gather.3 = bf16[2,8192]{1,0:T(2,128)(2,1)S(1)} all-gather(bf16[2,1024]{1,0:T(2,128)(2,1)S(1)} %pad_maximum_fusion.2), channel_id=1, replica_groups=mesh['rows'=4,'feat'=8] {'feat'}, dimensions={1}, use_global_device_ids=true | all-gather | bytes 36864 | tf_op jit(solution)/shard_map/all_gather | solution.py:171
  115.4 202.8 %while.11 = (s32[]{:T(128)}, f32[256,18,128]{0,1,2:T(8,128)}, bf16[8,18,1024]{2,1,0:T(8,128)(2,1)S(1)}, s32[8,128,1024]{1,2,0:T(8,128)}, s32[]{:T(128)}, /*index=5*/s32[]{:T(128)}) while((s32[]{:T(128)}, f32[256,18,128]{0,1,2:T(8,128)}, bf16[8,18,1024]{2,1,0:T(8,128)(2,1)S(1)}, s32[8,128,1024]{1,2,0:T(8,128)}, s32[]{:T(128)}, ...), condition=%wide.region_9.10_spmd.clone, body=%wide.region_8.9_spmd.clone.sunk | while | flops 1242693632 | bytes 7389279 | solution.py:110
  115.6 1.1 constant_dynamic-slice_fusion.2
  116.9 23.1 %bitcast_add_fusion.2 = f32[256,18,128]{0,1,2:T(8,128)} fusion(f32[256,18,128]{0,1,2:T(8,128)} %get-tuple-element.137, s32[128,1024]{1,0:T(8,128)S(1)} %bitcast.63, pred[]{:T(512)S(6)} %compare.9, bf16[8,18,1024]{2,1,0:T(8,128)(2,1)S(1)} %get-tuple-element.144, s32[]{:T(128)S(6)} %copy.29), kind=kOutput, calls=%fused_computation.4.clone.1 | convolution fusion | flops 1242693632 | bytes 5292037 | tf_op jit(solution)/shard_map/while/body/eval_jaxpr/fkr,cr->kcf/dot_general | solution.py:105
  140.0 1.1 constant_dynamic-slice_fusion.2
  141.3 24.2 %bitcast_add_fusion.2 = f32[256,18,128]{0,1,2:T(8,128)} fusion(f32[256,18,128]{0,1,2:T(8,128)} %get-tuple-element.137, s32[128,1024]{1,0:T(8,128)S(1)} %bitcast.63, pred[]{:T(512)S(6)} %compare.9, bf16[8,18,1024]{2,1,0:T(8,128)(2,1)S(1)} %get-tuple-element.144, s32[]{:T(128)S(6)} %copy.29), kind=kOutput, calls=%fused_computation.4.clone.1 | convolution fusion | flops 1242693632 | bytes 5292037 | tf_op jit(solution)/shard_map/while/body/eval_jaxpr/fkr,cr->kcf/dot_general | solution.py:105
  165.4 1.1 constant_dynamic-slice_fusion.2
  166.7 24.2 %bitcast_add_fusion.2 = f32[256,18,128]{0,1,2:T(8,128)} fusion(f32[256,18,128]{0,1,2:T(8,128)} %get-tuple-element.137, s32[128,1024]{1,0:T(8,128)S(1)} %bitcast.63, pred[]{:T(512)S(6)} %compare.9, bf16[8,18,1024]{2,1,0:T(8,128)(2,1)S(1)} %get-tuple-element.144, s32[]{:T(128)S(6)} %copy.29), kind=kOutput, calls=%fused_computation.4.clone.1 | convolution fusion | flops 1242693632 | bytes 5292037 | tf_op jit(solution)/shard_map/while/body/eval_jaxpr/fkr,cr->kcf/dot_general | solution.py:105
  190.9 1.1 constant_dynamic-slice_fusion.2
  192.2 24.2 %bitcast_add_fusion.2 = f32[256,18,128]{0,1,2:T(8,128)} fusion(f32[256,18,128]{0,1,2:T(8,128)} %get-tuple-element.137, s32[128,1024]{1,0:T(8,128)S(1)} %bitcast.63, pred[]{:T(512)S(6)} %compare.9, bf16[8,18,1024]{2,1,0:T(8,128)(2,1)S(1)} %get-tuple-element.144, s32[]{:T(128)S(6)} %copy.29), kind=kOutput, calls=%fused_computation.4.clone.1 | convolution fusion | flops 1242693632 | bytes 5292037 | tf_op jit(solution)/shard_map/while/body/eval_jaxpr/fkr,cr->kcf/dot_general | solution.py:105
  217.6 24.2 %bitcast_add_fusion.2 = f32[256,18,128]{0,1,2:T(8,128)} fusion(f32[256,18,128]{0,1,2:T(8,128)} %get-tuple-element.137, s32[128,1024]{1,0:T(8,128)S(1)} %bitcast.63, pred[]{:T(512)S(6)} %compare.9, bf16[8,18,1024]{2,1,0:T(8,128)(2,1)S(1)} %get-tuple-element.144, s32[]{:T(128)S(6)} %copy.29), kind=kOutput, calls=%fused_computation.4.clone.1 | convolution fusion | flops 1242693632 | bytes 5292037 | tf_op jit(solution)/shard_map/while/body/eval_jaxpr/fkr,cr->kcf/dot_general | solution.py:105
  243.1 24.2 %bitcast_add_fusion.2 = f32[256,18,128]{0,1,2:T(8,128)} fusion(f32[256,18,128]{0,1,2:T(8,128)} %get-tuple-element.137, s32[128,1024]{1,0:T(8,128)S(1)} %bitcast.63, pred[]{:T(512)S(6)} %compare.9, bf16[8,18,1024]{2,1,0:T(8,128)(2,1)S(1)} %get-tuple-element.144, s32[]{:T(128)S(6)} %copy.29), kind=kOutput, calls=%fused_computation.4.clone.1 | convolution fusion | flops 1242693632 | bytes 5292037 | tf_op jit(solution)/shard_map/while/body/eval_jaxpr/fkr,cr->kcf/dot_general | solution.py:105
  268.5 24.2 %bitcast_add_fusion.2 = f32[256,18,128]{0,1,2:T(8,128)} fusion(f32[256,18,128]{0,1,2:T(8,128)} %get-tuple-element.137, s32[128,1024]{1,0:T(8,128)S(1)} %bitcast.63, pred[]{:T(512)S(6)} %compare.9, bf16[8,18,1024]{2,1,0:T(8,128)(2,1)S(1)} %get-tuple-element.144, s32[]{:T(128)S(6)} %copy.29), kind=kOutput, calls=%fused_computation.4.clone.1 | convolution fusion | flops 1242693632 | bytes 5292037 | tf_op jit(solution)/shard_map/while/body/eval_jaxpr/fkr,cr->kcf/dot_general | solution.py:105
  292.7 1.1 constant_dynamic-slice_fusion.2
  294.0 24.2 %bitcast_add_fusion.2 = f32[256,18,128]{0,1,2:T(8,128)} fusion(f32[256,18,128]{0,1,2:T(8,128)} %get-tuple-element.137, s32[128,1024]{1,0:T(8,128)S(1)} %bitcast.63, pred[]{:T(512)S(6)} %compare.9, bf16[8,18,1024]{2,1,0:T(8,128)(2,1)S(1)} %get-tuple-element.144, s32[]{:T(128)S(6)} %copy.29), kind=kOutput, calls=%fused_computation.4.clone.1 | convolution fusion | flops 1242693632 | bytes 5292037 | tf_op jit(solution)/shard_map/while/body/eval_jaxpr/fkr,cr->kcf/dot_general | solution.py:105
  318.1 2.9 copy.21
  321.7 28.7 %reduce-scatter.2.cloned.1.call-done = bf16[64,18,128]{2,0,1:T(8,128)(2,1)} async-done(((bf16[256,18,128]{2,0,1:T(8,128)(2,1)}), bf16[64,18,128]{2,0,1:T(8,128)(2,1)}) %reduce-scatter.2.cloned.1.call-update) | async-done | bytes 294928 | tf_op jit(solution)/shard_map/reduce_scatter | solution.py:177
  (70 shorter events, 21.7 us)
Async XLA Ops:
  7.2 343.2 %reduce-scatter.2.cloned.1.call-start = ((), (), s32[]{:S(2)}) async-start(), calls=%async_computation.1 | async-start | bytes 1474560 | tf_op jit(solution)/shard_map/reduce_scatter | solution.py:177
  11.1 14.2 %collective-permute-start = (bf16[7,512]{1,0:T(8,128)(2,1)S(1)}, bf16[7,512]{1,0:T(8,128)(2,1)S(1)}, u32[]{:S(2)}, u32[]{:S(2)}) collective-permute-start(bf16[7,512]{1,0:T(8,128)(2,1)S(1)} %get-tuple-element.79), channel_id=1, source_target_pairs={{0,8},{8,16},{16,24},{1,9},{9,17},{17,25},{2,10},{10,18},{18,26},{... | collective-permute-start | bytes 21512 | tf_op jit(solution)/shard_map/ppermute | solution.py:25
  15.9 9.4 %collective-permute-start.1 = (bf16[7,512]{1,0:T(8,128)(2,1)S(1)}, bf16[7,512]{1,0:T(8,128)(2,1)S(1)}, u32[]{:S(2)}, u32[]{:S(2)}) collective-permute-start(bf16[7,512]{1,0:T(8,128)(2,1)S(1)} %get-tuple-element.80), channel_id=1, source_target_pairs={{8,0},{16,8},{24,16},{9,1},{17,9},{25,17},{10,2},{18,10},{26,18},{... | collective-permute-start | bytes 21512 | tf_op jit(solution)/shard_map/ppermute | solution.py:27
Sparse Core Ops, SparseCore 0:
  321.2 29.0 reduce-scatter.1
where the time goes:
time: 363 us; the launch traced here: 362 us
  matrix products  208 us (57%)
  blocking collectives  55.8 us (15%)
  waiting for transfers between devices  28.7 us (8%)
  local copies, waits for them, and re-layouts  23.9 us (7%)
  other arithmetic  21.8 us (6%)
  between operations  16.9 us (5%)
  starting transfers between devices  6.17 us (2%)
    dot_general x8, matrix products, add_block(): jnp.einsum('fkr,cr->kcf', onehot, column_piece, preferred_element_type=jn...  192 us
    psum x1, blocking collectives, per_device(): lax.psum(precise_dot(own_table.T, precise_dot(losses, far_table)), ('rows...  41.8 us
    reduce_scatter x1, waiting for transfers between devices, per_device(): lax.psum_scatter(bin_term(bins, columns, bins_dev * lax.axis_size('rows')...  28.7 us
    dot_general x7, matrix products, precise_dot(): return jnp.dot(left, right, precision=lax.Precision.HIGHEST)  15.7 us
    all_gather x1, blocking collectives, per_device(): grad_hess = lax.all_gather(pieces, 'feat', axis=1, tiled=True)  14 us
    reduce_sum x1, other arithmetic, lambdas(): jnp.sum((1.0 - ahead_prob) * weight_bwd - ahead_prob * weight_fwd, axis=1)  12.1 us
    dynamic_slice x16, local copies, waits for them, and re-layouts, bin_term(): running, _ = lax.scan(add_block, start_value, (bin_blocks, column_blocks))  10.2 us
    unnamed x5, local copies, waits for them, and re-layouts  8.19 us
  transfers between devices with their start and end apart: 3, of which 1 were waited for; matrix products, arithmetic and copies ran while one was open for 2% of the time, Pallas kernels for 0%

commit v1 on v0

--- a/solution.py
+++ b/solution.py
@@ -3,6 +3,8 @@
 import jax
 import jax.numpy as jnp
 from jax import lax
+from jax.experimental import pallas as pl
+from jax.experimental.pallas import tpu as pltpu
 from jax.sharding import PartitionSpec as P
 
 BINS = 256
@@ -88,27 +90,97 @@
     return (channels[:, None, :] * member[None, :, :]).reshape(3 * node_count, -1)
 
 
+FINE = 4
+GROUP = 4
+FEATURE_BLOCK = 8
+
+
+def hist_kernel(columns_ref, bins_ref, out_ref, total):
+    row_count = bins_ref.shape[1]
+    fine_columns = columns_ref.shape[0]
+    coarse = out_ref.shape[1]
+    chunk = math.gcd(1024, row_count)
+    total[...] = jnp.zeros_like(total)
+    tile_ids = lax.broadcasted_iota(jnp.int32, (16, chunk), 0).astype(jnp.float32)
+    fine_ids = lax.broadcasted_iota(jnp.int32, (fine_columns, chunk), 0) // (
+        fine_columns // FINE
+    )
+    fine_ids = fine_ids.astype(jnp.float32).astype(jnp.bfloat16)
+    one = jnp.ones((), jnp.bfloat16)
+    zero = jnp.zeros((), jnp.bfloat16)
+
+    def add_chunk(index, carry):
+        rows = pl.ds(pl.multiple_of(index * chunk, chunk), chunk)
+        values = bins_ref[:, rows]
+        high = (values >> 2).astype(jnp.float32)
+        low = (values & 3).astype(jnp.float32)
+        columns = columns_ref[:, rows]
+        for group in range(FEATURE_BLOCK // GROUP):
+            left, right = [], []
+            for member in range(GROUP):
+                feature = group * GROUP + member
+                high_row = jnp.broadcast_to(high[feature : feature + 1], (16, chunk)).astype(
+                    jnp.bfloat16
+                )
+                low_row = jnp.broadcast_to(low[feature : feature + 1], (16, chunk)).astype(
+                    jnp.bfloat16
+                )
+                for tile in range(coarse // 16):
+                    ids = (tile_ids + 16.0 * tile).astype(jnp.bfloat16)
+                    left.append(jnp.where(high_row == ids, one, zero))
+                for tile in range(fine_columns // 16):
+                    part = slice(16 * tile, 16 * tile + 16)
+                    right.append(jnp.where(low_row == fine_ids[part], columns[part], zero))
+            total[group] += lax.dot_general(
+                jnp.concatenate(left, axis=0),
+                jnp.concatenate(right, axis=0),
+                (((1,), (1,)), ((), ())),
+                preferred_element_type=jnp.float32,
+            )
+        return carry
+
+    lax.fori_loop(0, row_count // chunk, add_chunk, 0)
+    for group in range(FEATURE_BLOCK // GROUP):
+        for member in range(GROUP):
+            out_ref[group * GROUP + member] = total[
+                group,
+                member * coarse : (member + 1) * coarse,
+                member * fine_columns : (member + 1) * fine_columns,
+            ]
+
+
 def bin_term(bins, columns, amount):
-    levels = jnp.arange(amount, dtype=jnp.int32)
     feature_count, row_count = bins.shape
-    stride = math.gcd(1024, row_count)
-    block_count = row_count // stride
     column_count = columns.shape[0]
-    bin_blocks = bins.reshape(feature_count, block_count, stride).transpose(1, 0, 2)
-    column_blocks = columns.reshape(column_count, block_count, stride).transpose(1, 0, 2)
-
-    def add_block(running, pieces):
-        bin_piece, column_piece = pieces
-        onehot = (bin_piece[:, None, :] == levels[None, :, None]).astype(jnp.bfloat16)
-        return (
-            running
-            + jnp.einsum("fkr,cr->kcf", onehot, column_piece, preferred_element_type=jnp.float32),
-            None,
-        )
-
-    start_value = jnp.zeros((amount, column_count, feature_count), jnp.float32)
-    running, _ = lax.scan(add_block, start_value, (bin_blocks, column_blocks))
-    return running
+    coarse = amount // FINE
+    fine_columns = FINE * column_count
+    spread_columns = jnp.tile(columns, (FINE, 1))
+    sums = pl.pallas_call(
+        hist_kernel,
+        grid=(feature_count // FEATURE_BLOCK,),
+        out_shape=jax.ShapeDtypeStruct((feature_count, coarse, fine_columns), jnp.float32),
+        in_specs=[
+            pl.BlockSpec((fine_columns, row_count), lambda i: (0, 0)),
+            pl.BlockSpec((FEATURE_BLOCK, row_count), lambda i: (i, 0)),
+        ],
+        out_specs=pl.BlockSpec((FEATURE_BLOCK, coarse, fine_columns), lambda i: (i, 0, 0)),
+        scratch_shapes=[
+            pltpu.VMEM(
+                (FEATURE_BLOCK // GROUP, GROUP * coarse, GROUP * fine_columns), jnp.float32
+            )
+        ],
+        compiler_params=pltpu.CompilerParams(vmem_limit_bytes=40 * 1024 * 1024),
+        cost_estimate=pl.CostEstimate(
+            flops=2 * feature_count * coarse * row_count * 256,
+            bytes_accessed=4 * feature_count * row_count,
+            transcendentals=0,
+        ),
+    )(spread_columns, bins)
+    return (
+        sums.astype(jnp.bfloat16)
+        .transpose(1, 2, 0)
+        .reshape(amount, column_count, feature_count)
+    )
 
 
 def exact_planes(scores, query_ids, positions, clicks):
@@ -170,18 +242,15 @@
     )
     grad_hess = lax.all_gather(pieces, "feat", axis=1, tiled=True)
     channels = jnp.concatenate([grad_hess, jnp.ones((1, rows_dev), jnp.bfloat16)], axis=0)
-    columns = jnp.concatenate(
-        [node_columns(channels, nodes, NODES), node_columns(channels, nodes // 2, NODES // 2)],
-        axis=0,
-    )
+    columns = node_columns(channels, nodes, NODES)
     summed = lax.psum_scatter(
-        bin_term(bins, columns, bins_dev * lax.axis_size("rows")).astype(jnp.bfloat16),
+        bin_term(bins, columns, bins_dev * lax.axis_size("rows")),
         "rows",
         scatter_dimension=0,
         tiled=True,
     ).astype(jnp.float32)
-    node_hist = summed[:, : 3 * NODES].reshape(-1, 3, NODES, feature_count)
-    parent_hist = summed[:, 3 * NODES :].reshape(-1, 3, NODES // 2, feature_count)
+    node_hist = summed.reshape(-1, 3, NODES, feature_count)
+    parent_hist = node_hist[:, :, 0::2] + node_hist[:, :, 1::2]
     bias_ratios = jnp.stack([plus_ratio, minus_ratio])
     return (bias_ratios, grad_hess, node_hist, parent_hist)
 

time: 363 us -> 218 us (0.60)
  matrix products: 208 us -> 15.7 us
  Pallas kernels: 0 us -> 62.7 us
  local copies, waits for them, and re-layouts: 23.9 us -> 9.73 us
    dot_general x8 -> x0, matrix products: 192 us -> none  [add_block(): jnp.einsum('fkr,cr->kcf', onehot, column_piece, preferred_element_type=jn...]
    pallas_call x0 -> x1, Pallas kernels: none -> 62.7 us  [bin_term(): pl.pallas_call(hist_kernel, grid=(feature_count // FEATURE_BLOCK,), out_s...]
    dynamic_slice x16 -> x0, local copies, waits for them, and re-layouts: 10.2 us -> none  [bin_term(): running, _ = lax.scan(add_block, start_value, (bin_blocks, column_blocks))]
  transfers between devices with their start and end apart: 3 -> 3, of which waited for: 1 -> 2; matrix products, arithmetic and copies ran while one was open for 2% -> 1% of each run, Pallas kernels for 0% -> 0%
where the time goes in v1:
time: 218 us; the launch traced here: 217 us
  Pallas kernels  62.7 us (29%)
  blocking collectives  54.3 us (25%)
  waiting for transfers between devices  29.4 us (13%)
  other arithmetic  22.3 us (10%)
  between operations  16.9 us (8%)
  matrix products  15.7 us (7%)
  local copies, waits for them, and re-layouts  9.73 us (4%)
  starting transfers between devices  6.17 us (3%)
    pallas_call x1, Pallas kernels, bin_term(): pl.pallas_call(hist_kernel, grid=(feature_count // FEATURE_BLOCK,), out_s...  62.7 us
    psum x1, blocking collectives, per_device(): lax.psum(precise_dot(own_table.T, precise_dot(losses, far_table)), ('rows...  40.1 us
    reduce_scatter x1, waiting for transfers between devices, per_device(): lax.psum_scatter(bin_term(bins, columns, bins_dev * lax.axis_size('rows')...  26.8 us
    dot_general x7, matrix products, precise_dot(): return jnp.dot(left, right, precision=lax.Precision.HIGHEST)  15.7 us
    all_gather x1, blocking collectives, per_device(): grad_hess = lax.all_gather(pieces, 'feat', axis=1, tiled=True)  14.2 us
    reduce_sum x1, other arithmetic, lambdas(): jnp.sum((1.0 - ahead_prob) * weight_bwd - ahead_prob * weight_fwd, axis=1)  12 us
    unnamed x5, local copies, waits for them, and re-layouts  5.45 us
    ppermute x1, starting transfers between devices, extended_2(): lax.ppermute(tail, axis, [(i, (i + 1) % count) for i in range(ends)])  4.84 us
  transfers between devices with their start and end apart: 3, of which 2 were waited for; matrix products, arithmetic and copies ran while one was open for 1% of the time, Pallas kernels for 0%

profile of v1, /device:TPU:0, one launch (start us, length us, event | category | flops | bytes accessed | tf_op | source)
XLA Modules:
  0.0 217.2 jit_solution(14337585721628357963)
XLA Ops:
  7.2 0.8 subtract_convert_fusion
  8.1 0.8 fusion.64
  9.0 0.8 fusion.63
  9.9 0.8 add_convert_fusion
  11.1 4.8 %collective-permute-start = (bf16[7,512]{1,0:T(8,128)(2,1)S(1)}, bf16[7,512]{1,0:T(8,128)(2,1)S(1)}, u32[]{:S(2)}, u32[]{:S(2)}) collective-permute-start(bf16[7,512]{1,0:T(8,128)(2,1)S(1)} %get-tuple-element.22), channel_id=1, source_target_pairs={{0,8},{8,16},{16,24},{1,9},{9,17},{17,25},{2,10},{10,18},{18,26},{... | collective-permute-start | bytes 21512 | tf_op jit(solution)/shard_map/ppermute | solution.py:27
  15.9 1.3 collective-permute-start.1
  17.2 0.8 fusion.40
  18.0 0.8 fusion.51
  18.9 2.6 %collective-permute-done.1 = bf16[7,512]{1,0:T(8,128)(2,1)S(1)} collective-permute-done((bf16[7,512]{1,0:T(8,128)(2,1)S(1)}, bf16[7,512]{1,0:T(8,128)(2,1)S(1)}, u32[]{:S(2)}, u32[]{:S(2)}) %collective-permute-start.1) | collective-permute-done | bytes 7200 | tf_op jit(solution)/shard_map/ppermute | solution.py:29
  21.9 1.8 select_reduce_fusion
  24.1 12.0 %fusion.14 = f32[1024,32]{0,1:T(8,128)S(1)} fusion(f32[2048]{0:T(1024)S(1)} %bitcast.62, f32[1024]{0:T(1024)S(1)} %bitcast.54, f32[1024]{0:T(1024)S(1)} %get-tuple-element.47, f32[2048]{0:T(1024)S(1)} %bitcast.65, f32[2048]{0:T(1024)S(1)} %bitcast.60, f32[1024]{0:T(1024)S(1)} %get-tuple-element.46, f32[2048]{0:T(1024)S(1)} %bitcast.67, ...), kind=kOutput, calls=%fused_computation.24 | convolution fusion | flops 841023488 | bytes 194560 | tf_op jit(solution)/shard_map/dot_general | solution.py:41
  36.6 40.1 %psum.7 = f32[32,32]{1,0:T(8,128)S(1)} all-reduce(f32[32,32]{1,0:T(8,128)S(1)} %fusion.35), channel_id=1, replica_groups=mesh['rows'=4,'feat'=8] {'rows','feat'}, use_global_device_ids=true, to_apply=%region_2.3 | all-reduce | flops 1024 | bytes 8192 | tf_op jit(solution)/shard_map/psum | solution.py:237
  78.6 0.7 fusion.66
  81.1 0.7 fusion.27
  83.0 12.0 %fusion.11 = (bf16[1024]{0:T(1024)(128)(2,1)S(1)}, bf16[1024]{0:T(1024)(128)(2,1)S(1)}) fusion(f32[2048]{0:T(1024)S(1)} %bitcast.68, f32[1024]{0:T(1024)S(1)} %bitcast.75, f32[1024]{0:T(1024)S(1)} %bitcast.81, f32[2048]{0:T(1024)S(1)} %bitcast.80, f32[2048]{0:T(1024)S(1)} %bitcast.70, f32[1024]{0:T(1024)S(1)} %broadcast_subtract_fusion.1, ...), kind=kLoop, calls=%fused_computation.16 | loop fusion | flops 56621056 | bytes 96256 | tf_op jit(solution)/shard_map/reduce_sum | solution.py:81
  95.1 14.2 %all_gather.3 = bf16[2,8192]{1,0:T(2,128)(2,1)S(1)} all-gather(bf16[2,1024]{1,0:T(2,128)(2,1)S(1)} %pad_maximum_fusion.2), channel_id=1, replica_groups=mesh['rows'=4,'feat'=8] {'feat'}, dimensions={1}, use_global_device_ids=true | all-gather | bytes 36864 | tf_op jit(solution)/shard_map/all_gather | solution.py:243
  109.9 2.2 %copy-done = s32[128,8192]{1,0:T(8,128)S(1)} copy-done((s32[128,8192]{1,0:T(8,128)S(1)}, s32[128,8192]{1,0:T(8,128)}, u32[]{:S(2)}) %copy-start) | copy-done | bytes 4194328
  112.1 62.7 %shard_map.93 = f32[128,64,48]{2,1,0:T(8,128)S(1)} custom-call(bf16[48,8192]{1,0:T(8,128)(2,1)S(1)} %tile.9.columns_ref, s32[128,8192]{1,0:T(8,128)S(1)} %copy-done), custom_call_target="tpu_custom_call" | custom-call | flops 34359738368 | bytes 4194304 | tf_op jit(solution)/shard_map/pallas_call | solution.py:158
  175.3 2.2 %copy.19 = bf16[64,48,128]{2,1,0:T(8,128)(2,1)S(1)} copy(bf16[64,48,128]{1,0,2:T(8,128)(2,1)S(1)} %convert_bitcast_fusion) | data formatting | bytes 1572864 | tf_op jit(solution)/shard_map/transpose | solution.py:181
  177.6 1.1 copy.20
  179.3 26.8 %reduce-scatter.2.cloned.1.call-done = bf16[64,12,128]{2,0,1:T(8,128)(2,1)} async-done(((bf16[256,12,128]{2,0,1:T(8,128)(2,1)}), bf16[64,12,128]{2,0,1:T(8,128)(2,1)}) %reduce-scatter.2.cloned.1.call-update) | async-done | bytes 196624 | tf_op jit(solution)/shard_map/reduce_scatter | solution.py:246
  206.1 1.8 copy.21
  207.9 1.0 convert.11
  208.9 0.8 copy.22
  (45 shorter events, 6.6 us)
Async XLA Ops:
  7.2 198.9 %reduce-scatter.2.cloned.1.call-start = ((), (), s32[]{:S(2)}) async-start(), calls=%async_computation.1 | async-start | bytes 983040 | tf_op jit(solution)/shard_map/reduce_scatter | solution.py:246
  11.1 7.8 %collective-permute-start = (bf16[7,512]{1,0:T(8,128)(2,1)S(1)}, bf16[7,512]{1,0:T(8,128)(2,1)S(1)}, u32[]{:S(2)}, u32[]{:S(2)}) collective-permute-start(bf16[7,512]{1,0:T(8,128)(2,1)S(1)} %get-tuple-element.22), channel_id=1, source_target_pairs={{0,8},{8,16},{16,24},{1,9},{9,17},{17,25},{2,10},{10,18},{18,26},{... | collective-permute-start | bytes 21512 | tf_op jit(solution)/shard_map/ppermute | solution.py:27
  15.9 5.5 %collective-permute-start.1 = (bf16[7,512]{1,0:T(8,128)(2,1)S(1)}, bf16[7,512]{1,0:T(8,128)(2,1)S(1)}, u32[]{:S(2)}, u32[]{:S(2)}) collective-permute-start(bf16[7,512]{1,0:T(8,128)(2,1)S(1)} %get-tuple-element.23), channel_id=1, source_target_pairs={{8,0},{16,8},{24,16},{9,1},{17,9},{25,17},{10,2},{18,10},{26,18},{... | collective-permute-start | bytes 21512 | tf_op jit(solution)/shard_map/ppermute | solution.py:29
  109.9 2.2 %copy-start = (s32[128,8192]{1,0:T(8,128)S(1)}, s32[128,8192]{1,0:T(8,128)}, u32[]{:S(2)}) copy-start(s32[128,8192]{1,0:T(8,128)} %bins_ref.1) | copy-start | bytes 12582916
Sparse Core Ops, SparseCore 0:
  178.8 27.2 reduce-scatter.1

commit v2 on v1

--- a/solution.py
+++ b/solution.py
@@ -183,6 +183,164 @@
     )
 
 
+def greet(axes):
+    barrier = pltpu.get_barrier_semaphore()
+    arrivals = 0
+    for axis in axes:
+        count = lax.axis_size(axis)
+        place = lax.axis_index(axis)
+        for step in range(1, count):
+            pl.semaphore_signal(
+                barrier,
+                inc=1,
+                device_id={axis: lax.rem(place + step, count)},
+                device_id_type=pl.DeviceIdType.MESH,
+            )
+        arrivals += count - 1
+    pl.semaphore_wait(barrier, arrivals)
+
+
+def exchange(axis, source_for, slots, send_sems, recv_sems):
+    count = lax.axis_size(axis)
+    place = lax.axis_index(axis)
+    copies = []
+    for step in range(1, count):
+        peer = lax.rem(place + step, count)
+        copy = pltpu.make_async_remote_copy(
+            src_ref=source_for(peer),
+            dst_ref=slots.at[place],
+            send_sem=send_sems.at[step],
+            recv_sem=recv_sems.at[step],
+            device_id={axis: peer},
+            device_id_type=pl.DeviceIdType.MESH,
+        )
+        copy.start()
+        copies.append(copy)
+    for copy in copies:
+        copy.wait()
+
+
+def slot_sum(slots, count):
+    running = slots[0].astype(jnp.float32)
+    for index in range(1, count):
+        running = running + slots[index].astype(jnp.float32)
+    return running
+
+
+def ratio_kernel(
+    local_ref,
+    plus_ref,
+    minus_ref,
+    feat_slots,
+    rows_part,
+    rows_slots,
+    feat_send,
+    feat_recv,
+    rows_send,
+    rows_recv,
+):
+    feat_slots[lax.axis_index("feat")] = local_ref[...]
+    greet(("feat", "rows"))
+    exchange("feat", lambda peer: local_ref, feat_slots, feat_send, feat_recv)
+    part = slot_sum(feat_slots, lax.axis_size("feat"))
+    rows_part[...] = part
+    rows_slots[lax.axis_index("rows")] = part
+    exchange("rows", lambda peer: rows_part, rows_slots, rows_send, rows_recv)
+    totals = slot_sum(rows_slots, lax.axis_size("rows"))
+    plus = bias_ratio(jnp.sum(totals, axis=1, keepdims=True))
+    plus_ref[...] = plus
+    minus_ref[...] = bias_ratio(jnp.sum(totals / plus, axis=0, keepdims=True))
+
+
+def shared_ratios(local):
+    feat, rows = lax.axis_size("feat"), lax.axis_size("rows")
+    shape = local.shape
+    plus, minus = pl.pallas_call(
+        ratio_kernel,
+        out_shape=(
+            jax.ShapeDtypeStruct((P_SIZE, 1), jnp.float32),
+            jax.ShapeDtypeStruct((1, P_SIZE), jnp.float32),
+        ),
+        in_specs=[pl.BlockSpec(memory_space=pltpu.VMEM)],
+        out_specs=(
+            pl.BlockSpec(memory_space=pltpu.VMEM),
+            pl.BlockSpec(memory_space=pltpu.VMEM),
+        ),
+        scratch_shapes=[
+            pltpu.VMEM((feat,) + shape, jnp.float32),
+            pltpu.VMEM(shape, jnp.float32),
+            pltpu.VMEM((rows,) + shape, jnp.float32),
+            pltpu.SemaphoreType.DMA((feat,)),
+            pltpu.SemaphoreType.DMA((feat,)),
+            pltpu.SemaphoreType.DMA((rows,)),
+            pltpu.SemaphoreType.DMA((rows,)),
+        ],
+        compiler_params=pltpu.CompilerParams(collective_id=0, has_side_effects=True),
+    )(local)
+    return plus[:, 0], minus[0]
+
+
+def gather_kernel(piece_ref, out_ref, slots, send_sems, recv_sems):
+    slots[lax.axis_index("feat")] = piece_ref[...]
+    greet(("feat",))
+    exchange("feat", lambda peer: piece_ref, slots, send_sems, recv_sems)
+    out_ref[...] = slots[...]
+
+
+def gather_feat(pieces):
+    feat = lax.axis_size("feat")
+    channel_count, block_rows = pieces.shape
+    lanes = math.gcd(128, block_rows)
+    shape = (channel_count * block_rows // lanes, lanes)
+    gathered = pl.pallas_call(
+        gather_kernel,
+        out_shape=jax.ShapeDtypeStruct((feat,) + shape, jnp.float32),
+        in_specs=[pl.BlockSpec(memory_space=pltpu.VMEM)],
+        out_specs=pl.BlockSpec(memory_space=pltpu.VMEM),
+        scratch_shapes=[
+            pltpu.VMEM((feat,) + shape, jnp.float32),
+            pltpu.SemaphoreType.DMA((feat,)),
+            pltpu.SemaphoreType.DMA((feat,)),
+        ],
+        compiler_params=pltpu.CompilerParams(collective_id=1, has_side_effects=True),
+    )(pieces.astype(jnp.float32).reshape(shape))
+    return (
+        gathered.reshape(feat, channel_count, block_rows)
+        .transpose(1, 0, 2)
+        .reshape(channel_count, feat * block_rows)
+        .astype(jnp.bfloat16)
+    )
+
+
+def scatter_kernel(sums_ref, out_ref, slots, send_sems, recv_sems):
+    place = lax.axis_index("rows")
+    slots[place] = sums_ref[place]
+    greet(("rows",))
+    exchange("rows", lambda peer: sums_ref.at[peer], slots, send_sems, recv_sems)
+    out_ref[...] = slot_sum(slots, lax.axis_size("rows"))
+
+
+def scatter_rows(sums):
+    rows = lax.axis_size("rows")
+    amount, column_count, feature_count = sums.shape
+    shape = (amount // rows * column_count, feature_count)
+    summed = pl.pallas_call(
+        scatter_kernel,
+        out_shape=jax.ShapeDtypeStruct(shape, jnp.float32),
+        in_specs=[pl.BlockSpec(memory_space=pltpu.VMEM)],
+        out_specs=pl.BlockSpec(memory_space=pltpu.VMEM),
+        scratch_shapes=[
+            pltpu.VMEM((rows,) + shape, jnp.bfloat16),
+            pltpu.SemaphoreType.DMA((rows,)),
+            pltpu.SemaphoreType.DMA((rows,)),
+        ],
+        compiler_params=pltpu.CompilerParams(
+            collective_id=2, has_side_effects=True, vmem_limit_bytes=32 * 1024 * 1024
+        ),
+    )(sums.reshape((rows,) + shape))
+    return summed
+
+
 def exact_planes(scores, query_ids, positions, clicks):
     query_plus = query_ids + 1
     score_high = scores.astype(jnp.bfloat16)
@@ -234,21 +392,16 @@
     losses = jax.nn.softplus(-spread) * change * forward
     own_table = place_table(own_rows[3])
     far_table = place_table(window[3])
-    totals = lax.psum(precise_dot(own_table.T, precise_dot(losses, far_table)), ("rows", "feat"))
-    plus_ratio = bias_ratio(jnp.sum(totals, axis=1))
-    minus_ratio = bias_ratio(precise_dot(1.0 / plus_ratio, totals))
+    plus_ratio, minus_ratio = shared_ratios(
+        precise_dot(own_table.T, precise_dot(losses, far_table))
+    )
     pieces = lambdas(
         spread, change, forward, backward, own_table, far_table, plus_ratio, minus_ratio
     )
-    grad_hess = lax.all_gather(pieces, "feat", axis=1, tiled=True)
+    grad_hess = gather_feat(pieces)
     channels = jnp.concatenate([grad_hess, jnp.ones((1, rows_dev), jnp.bfloat16)], axis=0)
     columns = node_columns(channels, nodes, NODES)
-    summed = lax.psum_scatter(
-        bin_term(bins, columns, bins_dev * lax.axis_size("rows")),
-        "rows",
-        scatter_dimension=0,
-        tiled=True,
-    ).astype(jnp.float32)
+    summed = scatter_rows(bin_term(bins, columns, bins_dev * lax.axis_size("rows")))
     node_hist = summed.reshape(-1, 3, NODES, feature_count)
     parent_hist = node_hist[:, :, 0::2] + node_hist[:, :, 1::2]
     bias_ratios = jnp.stack([plus_ratio, minus_ratio])

time: 218 us -> 155 us (0.71)
  blocking collectives: 54.3 us -> 0 us
  Pallas kernels: 62.7 us -> 95.2 us
  waiting for transfers between devices: 29.4 us -> 2.6 us
  between operations: 16.9 us -> 0.96 us
    psum x1 -> x0, blocking collectives: 40.1 us -> none  [per_device(): lax.psum(precise_dot(own_table.T, precise_dot(losses, far_table)), ('rows...]
    pallas_call x0 -> x3, Pallas kernels: none -> 32.5 us  [the longest x1 13 us: shared_ratios(): pl.pallas_call(ratio_kernel, out_shape=(jax.ShapeDtypeStruct((P_SIZE, 1),...]
    reduce_scatter x1 -> x0, waiting for transfers between devices: 26.8 us -> none  [per_device(): lax.psum_scatter(bin_term(bins, columns, bins_dev * lax.axis_size('rows')...]
    all_gather x1 -> x0, blocking collectives: 14.2 us -> none  [per_device(): grad_hess = lax.all_gather(pieces, 'feat', axis=1, tiled=True)]
    slice x0 -> x2, local copies, waits for them, and re-layouts: none -> 2.77 us  [per_device(): parent_hist = node_hist[:, :, 0::2] + node_hist[:, :, 1::2]]
    unnamed x5 -> x7, local copies, waits for them, and re-layouts: 5.45 us -> 2.94 us
    dot_general x7 -> x6, matrix products: 15.7 us -> 16.8 us  [precise_dot(): return jnp.dot(left, right, precision=lax.Precision.HIGHEST)]
  transfers between devices with their start and end apart: 3 -> 2, of which waited for: 2 -> 1; matrix products, arithmetic and copies ran while one was open for 1% -> 1% of each run, Pallas kernels for 0% -> 0%
where the time goes in v2:
time: 155 us; the launch traced here: 154 us
  Pallas kernels  95.2 us (61%)
  other arithmetic  23.2 us (15%)
  matrix products  16.8 us (11%)
  local copies, waits for them, and re-layouts  9.36 us (6%)
  starting transfers between devices  6.13 us (4%)
  waiting for transfers between devices  2.6 us (2%)
    pallas_call x1, Pallas kernels, bin_term(): pl.pallas_call(hist_kernel, grid=(feature_count // FEATURE_BLOCK,), out_s...  62.7 us
    dot_general x6, matrix products, precise_dot(): return jnp.dot(left, right, precision=lax.Precision.HIGHEST)  16.8 us
    pallas_call x1, Pallas kernels, shared_ratios(): pl.pallas_call(ratio_kernel, out_shape=(jax.ShapeDtypeStruct((P_SIZE, 1),...  13 us
    pallas_call x1, Pallas kernels, scatter_rows(): pl.pallas_call(scatter_kernel, out_shape=jax.ShapeDtypeStruct(shape, jnp....  12.1 us
    reduce_sum x1, other arithmetic, lambdas(): jnp.sum((1.0 - ahead_prob) * weight_bwd - ahead_prob * weight_fwd, axis=1)  12 us
    pallas_call x1, Pallas kernels, gather_feat(): pl.pallas_call(gather_kernel, out_shape=jax.ShapeDtypeStruct((feat,) + sh...  7.39 us
    ppermute x1, starting transfers between devices, extended_2(): lax.ppermute(tail, axis, [(i, (i + 1) % count) for i in range(ends)])  4.84 us
  transfers between devices with their start and end apart: 2, of which 1 were waited for; matrix products, arithmetic and copies ran while one was open for 1% of the time, Pallas kernels for 0%

profile of v2, /device:TPU:0, one launch (start us, length us, event | category | flops | bytes accessed | tf_op | source)
XLA Modules:
  0.0 154.2 jit_solution(13547398405040698083)
XLA Ops:
  0.6 0.8 subtract_convert_fusion
  1.6 0.8 fusion.60
  2.4 0.8 fusion.59
  3.3 0.8 add_convert_fusion
  4.5 4.8 %collective-permute-start = (bf16[7,512]{1,0:T(8,128)(2,1)S(1)}, bf16[7,512]{1,0:T(8,128)(2,1)S(1)}, u32[]{:S(2)}, u32[]{:S(2)}) collective-permute-start(bf16[7,512]{1,0:T(8,128)(2,1)S(1)} %get-tuple-element.12), channel_id=1, source_target_pairs={{0,8},{8,16},{16,24},{1,9},{9,17},{17,25},{2,10},{10,18},{18,26},{... | collective-permute-start | bytes 21512 | tf_op jit(solution)/shard_map/ppermute | solution.py:27
  9.3 1.3 collective-permute-start.1
  10.6 0.8 fusion.40
  12.3 2.6 %collective-permute-done.1 = bf16[7,512]{1,0:T(8,128)(2,1)S(1)} collective-permute-done((bf16[7,512]{1,0:T(8,128)(2,1)S(1)}, bf16[7,512]{1,0:T(8,128)(2,1)S(1)}, u32[]{:S(2)}, u32[]{:S(2)}) %collective-permute-start.1) | collective-permute-done | bytes 7200 | tf_op jit(solution)/shard_map/ppermute | solution.py:29
  15.3 1.8 %select_reduce_fusion = f32[1024]{0:T(1024)S(1)} fusion(f32[2048]{0:T(1024)S(1)} %bitcast.65, f32[2048]{0:T(1024)S(1)} %bitcast.60, f32[1024]{0:T(1024)S(1)} %bitcast.72, pred[2048]{0:T(1024)(128)(4,1)S(1)} %compare_reduce_fusion), kind=kLoop, calls=%fused_computation.22 | loop fusion | flops 8387584 | bytes 26624 | tf_op jit(solution)/shard_map/reduce_sum | solution.py:52
  17.5 12.0 %fusion.14 = f32[1024,32]{0,1:T(8,128)S(1)} fusion(f32[2048]{0:T(1024)S(1)} %bitcast.58, f32[1024]{0:T(1024)S(1)} %bitcast.50, f32[1024]{0:T(1024)S(1)} %get-tuple-element.35, f32[2048]{0:T(1024)S(1)} %bitcast.61, f32[2048]{0:T(1024)S(1)} %bitcast.56, f32[1024]{0:T(1024)S(1)} %get-tuple-element.34, f32[2048]{0:T(1024)S(1)} %bitcast.63, ...), kind=kOutput, calls=%fused_computation.24 | convolution fusion | flops 841023488 | bytes 194560 | tf_op jit(solution)/shard_map/dot_general | solution.py:41
  29.5 1.2 fusion.35.local_ref
  30.7 13.0 %shard_map.93 = (f32[32,1]{1,0:T(8,128)}, f32[1,32]{1,0:T(1,128)}) custom-call(f32[32,32]{1,0:T(8,128)} %fusion.35.local_ref), custom_call_target="tpu_custom_call" | custom-call | tf_op jit(solution)/shard_map/pallas_call | solution.py:258
  43.7 1.1 fusion.33
  44.7 1.4 fusion.27
  46.1 0.8 reduce.1
  48.1 12.0 %fusion.11 = (bf16[1024]{0:T(1024)(128)(2,1)S(1)}, bf16[1024]{0:T(1024)(128)(2,1)S(1)}) fusion(f32[2048]{0:T(1024)S(1)} %bitcast.64, f32[1024]{0:T(1024)S(1)} %bitcast.71, f32[1024]{0:T(1024)S(1)} %bitcast.78, f32[2048]{0:T(1024)S(1)} %bitcast.77, f32[2048]{0:T(1024)S(1)} %bitcast.66, f32[1024]{0:T(1024)S(1)} %broadcast_subtract_fusion.1, ...), kind=kLoop, calls=%fused_computation.16 | loop fusion | flops 56621056 | bytes 96256 | tf_op jit(solution)/shard_map/reduce_sum | solution.py:81
  60.8 7.4 %shard_map.94 = f32[8,16,128]{2,1,0:T(8,128)} custom-call(f32[16,128]{1,0:T(8,128)} %reshape.92.piece_ref), custom_call_target="tpu_custom_call" | custom-call | tf_op jit(solution)/shard_map/pallas_call | solution.py:295
  68.2 0.8 convert_element_type.89
  69.6 2.2 %copy-done = s32[128,8192]{1,0:T(8,128)S(1)} copy-done((s32[128,8192]{1,0:T(8,128)S(1)}, s32[128,8192]{1,0:T(8,128)}, u32[]{:S(2)}) %copy-start) | copy-done | bytes 4194328
  71.8 62.7 %shard_map.95 = f32[128,64,48]{2,1,0:T(8,128)S(1)} custom-call(bf16[48,8192]{1,0:T(8,128)(2,1)S(1)} %tile.9.columns_ref, s32[128,8192]{1,0:T(8,128)S(1)} %copy-done), custom_call_target="tpu_custom_call" | custom-call | flops 34359738368 | bytes 4194304 | tf_op jit(solution)/shard_map/pallas_call | solution.py:158
  135.0 2.2 %copy.15 = bf16[64,48,128]{2,1,0:T(8,128)(2,1)S(1)} copy(bf16[64,48,128]{1,0,2:T(8,128)(2,1)S(1)} %convert_bitcast_fusion) | data formatting | bytes 1572864 | tf_op jit(solution)/shard_map/transpose | solution.py:181
  137.2 12.1 %shard_map.96 = f32[768,128]{1,0:T(8,128)S(1)} custom-call(bf16[4,768,128]{2,1,0:T(8,128)(2,1)S(1)} %bitcast.42), custom_call_target="tpu_custom_call" | custom-call | tf_op jit(solution)/shard_map/pallas_call | solution.py:327
  149.3 1.4 slice.79
  150.7 1.4 slice.78
  (42 shorter events, 7.0 us)
Async XLA Ops:
  4.5 7.8 %collective-permute-start = (bf16[7,512]{1,0:T(8,128)(2,1)S(1)}, bf16[7,512]{1,0:T(8,128)(2,1)S(1)}, u32[]{:S(2)}, u32[]{:S(2)}) collective-permute-start(bf16[7,512]{1,0:T(8,128)(2,1)S(1)} %get-tuple-element.12), channel_id=1, source_target_pairs={{0,8},{8,16},{16,24},{1,9},{9,17},{17,25},{2,10},{10,18},{18,26},{... | collective-permute-start | bytes 21512 | tf_op jit(solution)/shard_map/ppermute | solution.py:27
  9.3 5.5 %collective-permute-start.1 = (bf16[7,512]{1,0:T(8,128)(2,1)S(1)}, bf16[7,512]{1,0:T(8,128)(2,1)S(1)}, u32[]{:S(2)}, u32[]{:S(2)}) collective-permute-start(bf16[7,512]{1,0:T(8,128)(2,1)S(1)} %get-tuple-element.13), channel_id=1, source_target_pairs={{8,0},{16,8},{24,16},{9,1},{17,9},{25,17},{10,2},{18,10},{26,18},{... | collective-permute-start | bytes 21512 | tf_op jit(solution)/shard_map/ppermute | solution.py:29
  69.1 65.4 %copy-start.1 = (bf16[8,2,1024]{2,1,0:T(2,128)(2,1)}, bf16[8,2,1024]{2,1,0:T(2,128)(2,1)S(1)}, u32[]{:S(2)}) copy-start(bf16[8,2,1024]{2,1,0:T(2,128)(2,1)S(1)} %convert_element_type.90) | copy-start | bytes 98308
  69.6 2.2 %copy-start = (s32[128,8192]{1,0:T(8,128)S(1)}, s32[128,8192]{1,0:T(8,128)}, u32[]{:S(2)}) copy-start(s32[128,8192]{1,0:T(8,128)} %bins_ref.1) | copy-start | bytes 12582916
  134.5 17.6 %copy-start.2 = (f32[1,32]{1,0:T(1,128)S(1)}, f32[1,32]{1,0:T(1,128)}, u32[]{:S(2)}) copy-start(f32[1,32]{1,0:T(1,128)} %get-tuple-element.7) | copy-start | bytes 388

commit v3 on v2

--- a/solution.py
+++ b/solution.py
@@ -48,21 +48,41 @@
 def pair_terms(own_rows, window):
     same_query = jnp.logical_and(
         own_rows[1][:, None] == window[1][None, :], window[1][None, :] > 0.5
-    ).astype(jnp.float32)
-    clicked = jnp.sum(same_query * window[2][None, :], axis=1)
+    )
+    clicked = jnp.sum(jnp.where(same_query, window[2][None, :], 0.0), axis=1)
     rank_values = jnp.arange(MAXQ, dtype=jnp.float32)
     ideal_gain = jnp.sum(
         jnp.where(rank_values[None, :] < clicked[:, None], discount(rank_values)[None, :], 0.0),
         axis=1,
     )
-    ideal_gain = jnp.maximum(ideal_gain, 1.0)
+    return jnp.maximum(ideal_gain, 1.0)
+
+
+def gap_terms(own_rows, window):
+    same_query = jnp.logical_and(
+        own_rows[1][:, None] == window[1][None, :], window[1][None, :] > 0.5
+    )
+    gap = jnp.abs(discount(own_rows[3])[:, None] - discount(window[3])[None, :])
+    return jnp.where(same_query, gap, 0.0)
+
+
+def loss_sums(own_rows, window, ideal_gain):
     spread = own_rows[0][:, None] - window[0][None, :]
-    change = (
-        jnp.abs(discount(own_rows[3])[:, None] - discount(window[3])[None, :]) / ideal_gain[:, None]
-    )
-    forward = same_query * own_rows[2][:, None] * (1.0 - window[2])[None, :]
-    backward = same_query * (1.0 - own_rows[2])[:, None] * window[2][None, :]
-    return (spread, change, forward, backward)
+    softplus = jnp.maximum(-spread, 0.0) + jnp.log1p(jnp.exp(-jnp.abs(spread)))
+    losses = softplus * gap_terms(own_rows, window)
+    own_table = place_table(own_rows[3]) * (own_rows[2] / ideal_gain)[:, None]
+    far_table = place_table(window[3]) * (1.0 - window[2])[:, None]
+    return precise_dot(own_table.T, precise_dot(losses, far_table))
+
+
+def tiles_of(own_rows, window):
+    block_rows = own_rows.shape[1]
+    tile = math.gcd(256, block_rows)
+    starts = range(0, block_rows, tile)
+    return (
+        jnp.stack([own_rows[:, i : i + tile] for i in starts]),
+        jnp.stack([window[:, i : i + tile + 2 * MAXQ] for i in starts]),
+    )
 
 
 def bias_ratio(sums):
@@ -70,16 +90,23 @@
     return (sums + middle + eps) / (2.0 * middle + eps)
 
 
-def lambdas(spread, change, forward, backward, own_table, far_table, plus_ratio, minus_ratio):
-    plus_own = precise_dot(own_table, plus_ratio)
-    minus_own = precise_dot(own_table, minus_ratio)
-    plus_far = precise_dot(far_table, plus_ratio)
-    minus_far = precise_dot(far_table, minus_ratio)
-    weight_fwd = change * forward / (plus_own[:, None] * minus_far[None, :])
-    weight_bwd = change * backward / (plus_far[None, :] * minus_own[:, None])
-    ahead_prob = jax.nn.sigmoid(-spread)
-    gradient = jnp.sum((1.0 - ahead_prob) * weight_bwd - ahead_prob * weight_fwd, axis=1)
-    hessian = jnp.sum(ahead_prob * (1.0 - ahead_prob) * (weight_fwd + weight_bwd), axis=1)
+def lambdas(own_rows, window, ideal_gain, plus_ratio, minus_ratio):
+    own_table = place_table(own_rows[3])
+    far_table = place_table(window[3])
+    own_clicked = own_rows[2] > 0.5
+    own_ratio = jnp.where(
+        own_clicked, precise_dot(own_table, plus_ratio), precise_dot(own_table, minus_ratio)
+    )
+    far_plus = window[2] / precise_dot(far_table, plus_ratio)
+    far_minus = (1.0 - window[2]) / precise_dot(far_table, minus_ratio)
+    side = jnp.where(own_clicked, 1.0, -1.0)
+    spread = (own_rows[0][:, None] - window[0][None, :]) * side[:, None]
+    far_weight = jnp.where(own_clicked[:, None], far_minus[None, :], far_plus[None, :])
+    rho = jax.nn.sigmoid(-spread)
+    terms = rho * (gap_terms(own_rows, window) * far_weight)
+    scale = 1.0 / (ideal_gain * own_ratio)
+    gradient = -side * scale * jnp.sum(terms, axis=1)
+    hessian = scale * jnp.sum((1.0 - rho) * terms, axis=1)
     return jnp.stack([gradient, hessian]).astype(jnp.bfloat16)
 
 
@@ -92,7 +119,7 @@
 
 FINE = 4
 GROUP = 4
-FEATURE_BLOCK = 8
+FEATURE_BLOCK = 16
 
 
 def hist_kernel(columns_ref, bins_ref, out_ref, total):
@@ -388,16 +415,15 @@
     first_row = lax.axis_index("feat") * block_rows
     own_rows = lax.dynamic_slice_in_dim(packed, first_row, block_rows, 1)
     window = lax.dynamic_slice_in_dim(extended, first_row, block_rows + 2 * MAXQ, 1)
-    spread, change, forward, backward = pair_terms(own_rows, window)
-    losses = jax.nn.softplus(-spread) * change * forward
-    own_table = place_table(own_rows[3])
-    far_table = place_table(window[3])
+    own_tiles, windows = tiles_of(own_rows, window)
+    ideal_gain = jax.vmap(pair_terms)(own_tiles, windows)
     plus_ratio, minus_ratio = shared_ratios(
-        precise_dot(own_table.T, precise_dot(losses, far_table))
-    )
-    pieces = lambdas(
-        spread, change, forward, backward, own_table, far_table, plus_ratio, minus_ratio
-    )
+        jnp.sum(jax.vmap(loss_sums)(own_tiles, windows, ideal_gain), axis=0)
+    )
+    pieces = jax.vmap(lambdas, in_axes=(0, 0, 0, None, None))(
+        own_tiles, windows, ideal_gain, plus_ratio, minus_ratio
+    )
+    pieces = pieces.transpose(1, 0, 2).reshape(2, block_rows)
     grad_hess = gather_feat(pieces)
     channels = jnp.concatenate([grad_hess, jnp.ones((1, rows_dev), jnp.bfloat16)], axis=0)
     columns = node_columns(channels, nodes, NODES)

time: 155 us -> 129 us (0.83)
  Pallas kernels: 95.2 us -> 81.4 us
  other arithmetic: 23.2 us -> 15.2 us
  matrix products: 16.8 us -> 12.1 us
    pallas_call x1, Pallas kernels: 62.7 us -> 48.9 us  [bin_term(): pl.pallas_call(hist_kernel, grid=(feature_count // FEATURE_BLOCK,), out_s...]
    reduce_sum x2, other arithmetic: 13.8 us -> 5.7 us  [the longest x1 4.5 us: lambdas(): gradient = -side * scale * jnp.sum(terms, axis=1)]
    dot_general x6, matrix products: 16.8 us -> 12.1 us  [precise_dot(): return jnp.dot(left, right, precision=lax.Precision.HIGHEST)]
where the time goes in v3:
time: 129 us; the launch traced here: 128 us
  Pallas kernels  81.4 us (63%)
  other arithmetic  15.2 us (12%)
  matrix products  12.1 us (9%)
  local copies, waits for them, and re-layouts  9.47 us (7%)
  starting transfers between devices  6.13 us (5%)
  waiting for transfers between devices  2.52 us (2%)
    pallas_call x1, Pallas kernels, bin_term(): pl.pallas_call(hist_kernel, grid=(feature_count // FEATURE_BLOCK,), out_s...  48.9 us
    pallas_call x1, Pallas kernels, shared_ratios(): pl.pallas_call(ratio_kernel, out_shape=(jax.ShapeDtypeStruct((P_SIZE, 1),...  13 us
    dot_general x6, matrix products, precise_dot(): return jnp.dot(left, right, precision=lax.Precision.HIGHEST)  12.1 us
    pallas_call x1, Pallas kernels, scatter_rows(): pl.pallas_call(scatter_kernel, out_shape=jax.ShapeDtypeStruct(shape, jnp....  12.1 us
    pallas_call x1, Pallas kernels, gather_feat(): pl.pallas_call(gather_kernel, out_shape=jax.ShapeDtypeStruct((feat,) + sh...  7.38 us
    ppermute x1, starting transfers between devices, extended_2(): lax.ppermute(tail, axis, [(i, (i + 1) % count) for i in range(ends)])  4.84 us
    reduce_sum x1, other arithmetic, lambdas(): gradient = -side * scale * jnp.sum(terms, axis=1)  4.5 us
    unnamed x9, local copies, waits for them, and re-layouts  2.95 us
  transfers between devices with their start and end apart: 2, of which 1 were waited for; matrix products, arithmetic and copies ran while one was open for 1% of the time, Pallas kernels for 0%

profile of v3, /device:TPU:0, one launch (start us, length us, event | category | flops | bytes accessed | tf_op | source)
XLA Modules:
  0.0 127.9 jit_solution(17251712283800691831)
XLA Ops:
  0.6 0.8 subtract_convert_fusion
  1.6 0.8 fusion.65
  2.4 0.8 fusion.64
  3.3 0.8 add_convert_fusion
  4.5 4.8 %collective-permute-start = (bf16[7,512]{1,0:T(8,128)(2,1)S(1)}, bf16[7,512]{1,0:T(8,128)(2,1)S(1)}, u32[]{:S(2)}, u32[]{:S(2)}) collective-permute-start(bf16[7,512]{1,0:T(8,128)(2,1)S(1)} %get-tuple-element.16), channel_id=1, source_target_pairs={{0,8},{8,16},{16,24},{1,9},{9,17},{17,25},{2,10},{10,18},{18,26},{... | collective-permute-start | bytes 21512 | tf_op jit(solution)/shard_map/ppermute | solution.py:27
  9.3 1.3 %collective-permute-start.1 = (bf16[7,512]{1,0:T(8,128)(2,1)S(1)}, bf16[7,512]{1,0:T(8,128)(2,1)S(1)}, u32[]{:S(2)}, u32[]{:S(2)}) collective-permute-start(bf16[7,512]{1,0:T(8,128)(2,1)S(1)} %get-tuple-element.17), channel_id=1, source_target_pairs={{8,0},{16,8},{24,16},{9,1},{17,9},{25,17},{10,2},{18,10},{26,18},{... | collective-permute-start | bytes 21512 | tf_op jit(solution)/shard_map/ppermute | solution.py:29
  10.6 0.8 fusion.32
  12.4 2.5 %collective-permute-done.1 = bf16[7,512]{1,0:T(8,128)(2,1)S(1)} collective-permute-done((bf16[7,512]{1,0:T(8,128)(2,1)S(1)}, bf16[7,512]{1,0:T(8,128)(2,1)S(1)}, u32[]{:S(2)}, u32[]{:S(2)}) %collective-permute-start.1) | collective-permute-done | bytes 7200 | tf_op jit(solution)/shard_map/ppermute | solution.py:29
  15.5 1.2 select_reduce_fusion
  17.1 9.0 %fusion.3 = f32[4,256,32]{1,2,0:T(8,128)S(1)} fusion(f32[4,1280]{1,0:T(4,128)S(1)} %get-tuple-element.22, f32[4,256]{1,0:T(4,128)S(1)} %get-tuple-element.39, f32[4,1280]{1,0:T(4,128)S(1)} %get-tuple-element.23, f32[4,256]{1,0:T(4,128)S(1)} %get-tuple-element.42, f32[4,1280]{1,0:T(4,128)S(1)} %get-tuple-element.24, f32[4,256]{1,0:T(4,128)S(1)} %get-tuple-element.43, ...), kind=kOutput, calls=%fused_computation.6 | convolution fusion | flops 519372800 | bytes 250880 | tf_op jit(solution)/shard_map/vmap()/dot_general | solution.py:41
  26.2 0.9 convolution_bitcast_fusion.local_ref
  27.0 13.0 %shard_map.93 = (f32[32,1]{1,0:T(8,128)}, f32[1,32]{1,0:T(1,128)}) custom-call(f32[32,32]{1,0:T(8,128)} %convolution_bitcast_fusion.local_ref), custom_call_target="tpu_custom_call" | custom-call | tf_op jit(solution)/shard_map/pallas_call | solution.py:285
  40.0 0.8 fusion.30
  40.8 1.0 fusion.23
  41.8 0.8 reduce
  43.1 4.5 %fusion.12 = (f32[4,256]{1,0:T(4,128)S(1)}, f32[4,256]{1,0:T(4,128)S(1)}) fusion(f32[4,1280]{1,0:T(4,128)S(1)} %get-tuple-element.19, f32[4,1280]{1,0:T(4,128)S(1)} %get-tuple-element.18, f32[4,256]{1,0:T(4,128)S(1)} %get-tuple-element.12, f32[4,1280]{1,0:T(4,128)S(1)} %get-tuple-element.22, f32[4,256]{1,0:T(4,128)S(1)} %get-tuple-element.39, ...), kind=kLoop, calls=%fused_computation.16 | loop fusion | flops 20969472 | bytes 133120 | tf_op jit(solution)/shard_map/vmap()/reduce_sum | solution.py:108
  48.3 7.4 %shard_map.94 = f32[8,16,128]{2,1,0:T(8,128)} custom-call(f32[16,128]{1,0:T(8,128)} %reshape.104.piece_ref), custom_call_target="tpu_custom_call" | custom-call | tf_op jit(solution)/shard_map/pallas_call | solution.py:322
  55.7 0.8 convert_element_type.91
  57.1 2.2 %copy-done = s32[128,8192]{1,0:T(8,128)S(1)} copy-done((s32[128,8192]{1,0:T(8,128)S(1)}, s32[128,8192]{1,0:T(8,128)}, u32[]{:S(2)}) %copy-start) | copy-done | bytes 4194328
  59.3 48.9 %shard_map.95 = f32[128,64,48]{2,1,0:T(8,128)S(1)} custom-call(bf16[48,8192]{1,0:T(8,128)(2,1)S(1)} %tile.9.columns_ref, s32[128,8192]{1,0:T(8,128)S(1)} %copy-done), custom_call_target="tpu_custom_call" | custom-call | flops 34359738368 | bytes 4194304 | tf_op jit(solution)/shard_map/pallas_call | solution.py:185
  108.7 2.2 %copy.33 = bf16[64,48,128]{2,1,0:T(8,128)(2,1)S(1)} copy(bf16[64,48,128]{1,0,2:T(8,128)(2,1)S(1)} %convert_bitcast_fusion) | data formatting | bytes 1572864 | tf_op jit(solution)/shard_map/transpose | solution.py:208
  110.9 12.1 %shard_map.96 = f32[768,128]{1,0:T(8,128)S(1)} custom-call(bf16[4,768,128]{2,1,0:T(8,128)(2,1)S(1)} %bitcast.98), custom_call_target="tpu_custom_call" | custom-call | tf_op jit(solution)/shard_map/pallas_call | solution.py:354
  123.0 1.4 %slice.124 = f32[64,3,2,128]{3,2,1,0:T(2,128)S(1)} slice(f32[64,3,4,128]{3,2,1,0:T(4,128)S(1)} %bitcast.95), slice={[0:64:1], [0:3:1], [1:4:2], [0:128:1]} | slice | bytes 393216 | tf_op jit(solution)/shard_map/slice | solution.py:432
  124.4 1.4 %slice.123 = f32[64,3,2,128]{3,2,1,0:T(2,128)S(1)} slice(f32[64,3,4,128]{3,2,1,0:T(4,128)S(1)} %bitcast.96), slice={[0:64:1], [0:3:1], [0:4:2], [0:128:1]} | slice | bytes 393216 | tf_op jit(solution)/shard_map/slice | solution.py:432
  (57 shorter events, 6.5 us)
Async XLA Ops:
  4.5 7.9 %collective-permute-start = (bf16[7,512]{1,0:T(8,128)(2,1)S(1)}, bf16[7,512]{1,0:T(8,128)(2,1)S(1)}, u32[]{:S(2)}, u32[]{:S(2)}) collective-permute-start(bf16[7,512]{1,0:T(8,128)(2,1)S(1)} %get-tuple-element.16), channel_id=1, source_target_pairs={{0,8},{8,16},{16,24},{1,9},{9,17},{17,25},{2,10},{10,18},{18,26},{... | collective-permute-start | bytes 21512 | tf_op jit(solution)/shard_map/ppermute | solution.py:27
  9.3 5.5 %collective-permute-start.1 = (bf16[7,512]{1,0:T(8,128)(2,1)S(1)}, bf16[7,512]{1,0:T(8,128)(2,1)S(1)}, u32[]{:S(2)}, u32[]{:S(2)}) collective-permute-start(bf16[7,512]{1,0:T(8,128)(2,1)S(1)} %get-tuple-element.17), channel_id=1, source_target_pairs={{8,0},{16,8},{24,16},{9,1},{17,9},{25,17},{10,2},{18,10},{26,18},{... | collective-permute-start | bytes 21512 | tf_op jit(solution)/shard_map/ppermute | solution.py:29
  56.6 51.6 %copy-start.1 = (bf16[8,2,1024]{2,1,0:T(2,128)(2,1)}, bf16[8,2,1024]{2,1,0:T(2,128)(2,1)S(1)}, u32[]{:S(2)}) copy-start(bf16[8,2,1024]{2,1,0:T(2,128)(2,1)S(1)} %convert_element_type.92) | copy-start | bytes 98308
  57.1 2.2 %copy-start = (s32[128,8192]{1,0:T(8,128)S(1)}, s32[128,8192]{1,0:T(8,128)}, u32[]{:S(2)}) copy-start(s32[128,8192]{1,0:T(8,128)} %bins_ref.1) | copy-start | bytes 12582916
  108.2 17.6 %copy-start.2 = (f32[1,32]{1,0:T(1,128)S(1)}, f32[1,32]{1,0:T(1,128)}, u32[]{:S(2)}) copy-start(f32[1,32]{1,0:T(1,128)} %get-tuple-element.7) | copy-start | bytes 388
